TPU v7x, 256 devices: a whole 4x4x8 slice. The times are simulated.
256 devices in a mesh: row: 8 (over y, core), col: 32 (over z, x).
Axes of the slice: x: 4, y: 4, z: 8, core: 2. Of those that a mesh axis runs over, the one named last changes fastest.
Arguments:
- sigma_top: float32 [8192, 8192], P('row', 'col')
- panel: float32 [4, 8192, 512], P(None, ('row', 'col')), may hold values from -0.0007324219 to 0.0007324219
- parent_panel: float32 [3, 512, 512], replicated, may hold values from -0.1875 to 0.1875
- diag_inverse: float32 [4, 512, 512], replicated, as said below
- block_depth: int32 [64], replicated, may hold values from 0 to 4, as said below
Outputs:
- sigma_cols: float32 [4, 8192, 512], P(None, ('row', 'col'))
- sigma_link: float32 [3, 512, 512], P(None, 'row')
- sigma_diag: float32 [4, 512, 512], P(None, 'row')
Inputs may be any that keep to these rules, and one draw needn't show every extreme that they name: Ancestor rows are nested: supernode k holds block b among its ancestor rows exactly when block_depth[b] > k. Each diag_inverse[k] is lower triangular. sigma_top is symmetric: sigma_top[i, j] = sigma_top[j, i] exactly.
All inputs are finite; a program needn't handle non-finite values.
Results may differ from a plain program's by a relative error of at most 0.0001.
Values sent between devices are 32-bit elements; how exact they have to be, the bound alone decides.
No kernel may reach another device: no remote copies, remote signals or barrier semaphores. Data moves between devices by JAX's collectives and lax.ppermute only.
A program may use at most 128 MiB of HBM per device.

v0:
```python
import jax
import jax.numpy as jnp
from jax import lax
from jax.sharding import PartitionSpec as P

STEPS = 4
BLOCK = 128


def broadcast(value, axis, root):
    mine = lax.axis_index(axis) == root
    return lax.psum(jnp.where(mine, value, jnp.zeros_like(value)), axis)


def row_depth(block_depth, first_row, row_total):
    blocks = (first_row + jnp.arange(row_total, dtype=jnp.int32)) // BLOCK
    block_ids = jnp.arange(block_depth.shape[0], dtype=jnp.int32)
    matched = (blocks[:, None] == block_ids[None, :]).astype(jnp.int32)
    return jnp.sum(matched * block_depth[None, :], axis=1)


def shards(sigma_top, panel, parent_panel, diag_inverse, block_depth):
    highest = lax.Precision.HIGHEST
    row_count = lax.axis_size("row")
    col_count = lax.axis_size("col")
    row_index = lax.axis_index("row")
    col_index = lax.axis_index("col")
    per_row = col_count // row_count
    share_rows = panel.shape[1]
    width = panel.shape[2]
    group_rows = sigma_top.shape[1]
    out_rows = width // row_count
    own_depth = row_depth(block_depth, (row_index * col_count + col_index) * share_rows, share_rows)
    col_depth = row_depth(block_depth, col_index * group_rows, group_rows)
    own_masks = []
    masked_list = []
    col_panels = []
    for section in range(STEPS):
        own_mask = jnp.where(own_depth > section, 1.0, 0.0).astype(jnp.float32)[:, None]
        col_mask = jnp.where(col_depth > section, 1.0, 0.0).astype(jnp.float32)[:, None]
        this_panel = panel[section]
        own_masks.append(own_mask)
        masked_list.append(own_mask * this_panel)
        row_group = lax.all_gather(this_panel, "col", axis=0, tiled=True)
        selected = lax.dynamic_slice_in_dim(
            row_group, col_index % per_row * group_rows, group_rows, 0
        )
        column_part = broadcast(selected, "row", col_index // per_row)
        col_panels.append(col_mask * column_part)
    products = []
    for section in range(STEPS):

        def panel_term(row_start, row_total, col_panel=col_panels[section]):
            return jnp.dot(
                sigma_top, col_panel, precision=highest, preferred_element_type=jnp.float32
            )

        products.append(
            lax.psum_scatter(
                panel_term(jnp.int32(0), share_rows * lax.axis_size("col")),
                "col",
                scatter_dimension=0,
                tiled=True,
            )
        )
    column_list = []
    cross_parts = []
    diag_parts = []
    for section in range(STEPS):
        summed = products[section]
        if section > 0:
            earlier = column_list[-1]
            cross_parts.append(jnp.dot(earlier.T, masked_list[section], precision=highest))
            summed = summed + jnp.dot(earlier, parent_panel[section - 1], precision=highest)
        current_cols = -own_masks[section] * summed
        column_list.append(current_cols)
        diag_parts.append(jnp.dot(masked_list[section].T, current_cols, precision=highest))
    link_list = []
    diagonals = []
    for section in range(STEPS):
        inverse = diag_inverse[section]
        offset = jnp.dot(inverse.T, inverse, precision=highest)
        if section > 0:
            parent = parent_panel[section - 1]
            crossed = lax.psum(cross_parts[section - 1], ("row", "col"))
            link_block = -(crossed + jnp.dot(diagonals[-1], parent, precision=highest))
            link_list.append(link_block)
            offset = offset - jnp.dot(parent.T, link_block, precision=highest)
        diagonals.append(offset - lax.psum(diag_parts[section], ("row", "col")))
    link_stack = lax.dynamic_slice_in_dim(jnp.stack(link_list), row_index * out_rows, out_rows, 1)
    diag_stack = lax.dynamic_slice_in_dim(jnp.stack(diagonals), row_index * out_rows, out_rows, 1)
    return (jnp.stack(column_list), link_stack, diag_stack)


def solution(mesh):
    return jax.shard_map(
        shards,
        mesh=mesh,
        in_specs=(P("row", "col"), P(None, ("row", "col"), None), P(), P(), P()),
        out_specs=(P(None, ("row", "col"), None), P(None, "row", None), P(None, "row", None)),
        check_vma=False,
    )
```

profile of v0, /device:TPU:44, one launch (start us, length us, event | category | flops | bytes accessed | tf_op | source)
XLA Modules:
  0.0 1584.5 jit_solution(3363226446138155626)
XLA Ops:
  7.2 0.0 all-gather.15.cloned.1.call-start
  7.2 1.7 fusion.86
  9.0 0.0 all-gather.13.cloned.1.call-start
  9.0 0.7 all-gather.13.cloned.1.call-update
  9.7 0.0 all-gather.11.cloned.1.call-start
  9.8 0.7 all-gather.11.cloned.1.call-update
  10.4 0.0 all-gather.9.cloned.1.call-start
  10.5 0.5 all-gather.9.cloned.1.call-update
  11.0 0.0 all-reduce.7.cloned.1.call-start
  11.1 78.7 %all-gather.15.cloned.1.call-done = f32[1,1024,512]{2,1,0:T(8,128)} async-done(((f32[1,32,512]{2,1,0:T(8,128)}), f32[1,1024,512]{2,1,0:T(8,128)}) %all-gather.15.cloned.1.call-update) | async-done | bytes 2097168 | tf_op jit(solution)/shard_map/all_gather | solution.py:44
  89.8 1.9 select_bitcast_fusion
  91.6 75.9 %all-gather.13.cloned.1.call-done = f32[1,1024,512]{2,1,0:T(8,128)} async-done(((f32[1,32,512]{2,1,0:T(8,128)}), f32[1,1024,512]{2,1,0:T(8,128)}) %all-gather.13.cloned.1.call-update) | async-done | bytes 2097168 | tf_op jit(solution)/shard_map/all_gather | solution.py:44
  167.5 1.9 select_bitcast_fusion.1
  169.4 76.4 %all-gather.11.cloned.1.call-done = f32[1,1024,512]{2,1,0:T(8,128)} async-done(((f32[1,32,512]{2,1,0:T(8,128)}), f32[1,1024,512]{2,1,0:T(8,128)}) %all-gather.11.cloned.1.call-update) | async-done | bytes 2097168 | tf_op jit(solution)/shard_map/all_gather | solution.py:44
  245.8 1.9 select_bitcast_fusion.2
  247.7 76.3 %all-gather.9.cloned.1.call-done = f32[1,1024,512]{2,1,0:T(8,128)} async-done(((f32[1,32,512]{2,1,0:T(8,128)}), f32[1,1024,512]{2,1,0:T(8,128)}) %all-gather.9.cloned.1.call-update) | async-done | bytes 2097168 | tf_op jit(solution)/shard_map/all_gather | solution.py:44
  324.0 1.9 select_bitcast_fusion.3
  325.9 0.0 reduce-scatter.13.cloned.1.call-start
  326.0 0.1 select_reduce_fusion
  326.1 68.7 %all-reduce.7.cloned.1.call-done = (f32[256,512]{1,0:T(8,128)}, f32[256,512]{1,0:T(8,128)}, f32[256,512]{1,0:T(8,128)}, f32[256,512]{1,0:T(8,128)}) async-done(((f32[256,512]{1,0:T(8,128)}, f32[256,512]{1,0:T(8,128)}, f32[256,512]{1,0:T(8,128)}, f32[256,512]{1,0:T(8,128)}), (f32[256,512]{1,0:T(8,128)}, f32[256,512]{1,0:T(8,128)}, f32[256,512]{1,0:T(8,128)}, ...) | async-done | bytes 2097168 | tf_op jit(solution)/shard_map/psum | solution.py:12
  394.7 4.6 convolution_bitcast_fusion.3
  399.3 1.8 copy.20
  401.2 0.0 reduce-scatter.15.cloned.1.call-start
  401.2 4.6 convolution_bitcast_fusion.2
  405.8 1.9 copy.22
  407.7 0.2 reduce-scatter.17.cloned.1.call-start
  407.9 4.6 convolution_bitcast_fusion.1
  412.5 1.8 copy.24
  414.4 0.0 reduce-scatter.19.cloned.1.call-start
  414.4 4.6 convolution_bitcast_fusion
  419.0 1.8 copy.26
  420.9 0.3 all-reduce.5.cloned.1.call-start
  421.2 0.2 select_reduce_fusion.1
  421.4 196.8 %reduce-scatter.13.cloned.1.call-done = f32[32,512]{1,0:T(8,128)} async-done(((f32[1024,512]{1,0:T(8,128)}), f32[32,512]{1,0:T(8,128)}) %reduce-scatter.13.cloned.1.call-update) | async-done | bytes 65552
  618.1 1.0 copy.21
  619.1 218.0 %reduce-scatter.15.cloned.1.call-done = f32[32,512]{1,0:T(8,128)} async-done(((f32[1024,512]{1,0:T(8,128)}), f32[32,512]{1,0:T(8,128)}) %reduce-scatter.15.cloned.1.call-update) | async-done | bytes 65552 | tf_op jit(solution)/shard_map/reduce_scatter | solution.py:59
  837.1 1.9 fusion.12
  839.0 2.1 fusion.65
  841.1 2.1 fusion.63
  843.1 212.3 %reduce-scatter.17.cloned.1.call-done = f32[32,512]{1,0:T(8,128)} async-done(((f32[1024,512]{1,0:T(8,128)}), f32[32,512]{1,0:T(8,128)}) %reduce-scatter.17.cloned.1.call-update) | async-done | bytes 65552 | tf_op jit(solution)/shard_map/reduce_scatter | solution.py:59
  1055.4 1.9 fusion.11
  1057.3 2.2 fusion.64
  1059.5 2.0 fusion.67
  1061.5 2.0 fusion.57
  1063.5 2.1 fusion.55
  1065.6 208.6 %reduce-scatter.19.cloned.1.call-done = f32[32,512]{1,0:T(8,128)} async-done(((f32[1024,512]{1,0:T(8,128)}), f32[32,512]{1,0:T(8,128)}) %reduce-scatter.19.cloned.1.call-update) | async-done | bytes 65552 | tf_op jit(solution)/shard_map/reduce_scatter | solution.py:59
  1274.3 1.9 fusion.10
  1276.2 2.1 fusion.66
  1278.3 4.4 fusion.17
  1282.8 3.4 fusion.15
  1286.2 3.7 fusion.13
  1289.9 0.7 multiply_bitcast_fusion
  1290.6 1.1 copy.19
  1291.7 1.6 pad_maximum_fusion
  1293.3 265.2 %all-reduce.5.cloned.1.call-done = (f32[512,512]{1,0:T(8,128)}, f32[512,512]{1,0:T(8,128)}, f32[512,512]{1,0:T(8,128)}, f32[512,512]{1,0:T(8,128)}, f32[512,512]...) async-done(((f32[512,512]{1,0:T(8,128)}, f32[512,512]{1,0:T(8,128)}, f32[512,512]{1,0:T(8,128)}, f32[512,512]{1,0:T(8,128)}, f32[512,512]{1,0:T(8,128)}, ...) | async-done | bytes 7340048 | tf_op jit(solution)/shard_map/psum | solution.py:85
  1558.4 3.9 convolution_subtract_fusion
  1562.3 3.1 fusion.9
  1565.5 1.9 fusion.8
  1567.5 1.9 fusion.6
  1569.4 2.0 fusion.5
  1571.4 2.2 fusion.3
  1573.6 2.0 fusion.2
  1575.6 0.8 fusion.50
  1576.4 0.8 fusion.44
  (33 shorter events, 0.2 us)
Async XLA Ops:
  7.2 387.6 %copy-start = (f32[1024,256]{1,0:T(8,128)S(1)}, f32[1024,256]{1,0:T(8,128)}, u32[]{:S(2)}) copy-start(f32[1024,256]{1,0:T(8,128)} %param.5) | copy-start | bytes 3145732
  7.2 82.6 %all-gather.15.cloned.1.call-start = ((), (), s32[]{:S(2)}) async-start(), calls=%async_computation.7 | async-start | bytes 2162688 | tf_op jit(solution)/shard_map/all_gather | solution.py:44
  9.0 158.5 %all-gather.13.cloned.1.call-start = ((), (), s32[]{:S(2)}) async-start(), calls=%async_computation.6 | async-start | bytes 2162688 | tf_op jit(solution)/shard_map/all_gather | solution.py:44
  9.7 236.1 %all-gather.11.cloned.1.call-start = ((), (), s32[]{:S(2)}) async-start(), calls=%async_computation.5 | async-start | bytes 2162688 | tf_op jit(solution)/shard_map/all_gather | solution.py:44
  10.4 313.5 %all-gather.9.cloned.1.call-start = ((), (), s32[]{:S(2)}) async-start(), calls=%async_computation.4 | async-start | bytes 2162688 | tf_op jit(solution)/shard_map/all_gather | solution.py:44
  11.0 383.7 %all-reduce.7.cloned.1.call-start = ((), (), s32[]{:S(2)}) async-start(), calls=%async_computation.13 | async-start | bytes 4194304 | tf_op jit(solution)/shard_map/psum | solution.py:12
  11.1 314.9 %copy-start.10 = (s32[64]{0:T(128)S(1)}, s32[64]{0:T(128)}, u32[]{:S(2)}) copy-start(s32[64]{0:T(128)} %param.9) | copy-start | bytes 772
  325.9 292.2 %reduce-scatter.13.cloned.1.call-start = ((), (), s32[]{:S(2)}) async-start(), calls=%async_computation.8 | async-start | bytes 2162688
  401.2 435.9 %reduce-scatter.15.cloned.1.call-start = ((), (), s32[]{:S(2)}) async-start(), calls=%async_computation.9 | async-start | bytes 2162688 | tf_op jit(solution)/shard_map/reduce_scatter | solution.py:59
  407.7 647.7 %reduce-scatter.17.cloned.1.call-start = ((), (), s32[]{:S(2)}) async-start(), calls=%async_computation.10 | async-start | bytes 2162688 | tf_op jit(solution)/shard_map/reduce_scatter | solution.py:59
  414.4 859.9 %reduce-scatter.19.cloned.1.call-start = ((), (), s32[]{:S(2)}) async-start(), calls=%async_computation.11 | async-start | bytes 2162688 | tf_op jit(solution)/shard_map/reduce_scatter | solution.py:59
  419.0 420.0 %copy-start.3 = (f32[4,32,512]{2,1,0:T(8,128)S(1)}, f32[4,32,512]{2,1,0:T(8,128)}, u32[]{:S(2)}) copy-start(f32[4,32,512]{2,1,0:T(8,128)} %param.6) | copy-start | bytes 786436
  420.9 1137.5 %all-reduce.5.cloned.1.call-start = ((), (), s32[]{:S(2)}) async-start(), calls=%async_computation.12 | async-start | bytes 14680064 | tf_op jit(solution)/shard_map/psum | solution.py:85
  1276.2 2.1 copy-start.9
  1558.4 3.9 copy-start.1
  1558.4 7.1 copy-start.2
  1558.4 7.1 copy-start.6
  1565.5 2.0 copy-start.8
  1567.5 1.9 copy-start.5
  1569.3 2.0 copy-start.7
  1571.4 2.2 copy-start.4
Sparse Core Ops, SparseCore 0:
  11.2 78.5 all-gather.14
  92.3 75.1 all-gather.12
  170.7 75.1 all-gather.10
  248.8 75.1 all-gather.8
  327.0 67.7 all-reduce.6
  401.3 216.7 reduce-scatter.12
  622.5 214.5 reduce-scatter.14
  840.9 214.4 reduce-scatter.16
  1059.7 214.4 reduce-scatter.18
  1280.5 277.8 all-reduce.4
where the time goes:
time: 1590 us; the launch traced here: 1580 us
  waiting for transfers between devices  1480 us (93%)
  matrix products  67.2 us (4%)
    reduce_scatter x3, waiting for transfers between devices, shards(): lax.psum_scatter(panel_term(jnp.int32(0), share_rows * lax.axis_size('col...  639 us
    all_gather x4, waiting for transfers between devices, shards(): row_group = lax.all_gather(this_panel, 'col', axis=0, tiled=True)  307 us
    psum x1, waiting for transfers between devices, shards(): crossed = lax.psum(cross_parts[section - 1], ('row', 'col'))  265 us
    unnamed x11, waiting for transfers between devices  199 us
    psum x1, waiting for transfers between devices, broadcast(): return lax.psum(jnp.where(mine, value, jnp.zeros_like(value)), axis)  68.7 us
  transfers between devices with their start and end apart: 10, of which 10 were waited for; matrix products, arithmetic and copies ran while one was open for 4% of the time, Pallas kernels for 0%

commit v1 on v0

v1 whole, which is shorter than its diff:
```python
import jax
import jax.numpy as jnp
from jax import lax
from jax.sharding import Mesh, PartitionSpec as P

BLOCK = 128
ROW = ("y", "core")
COL = ("z", "x")
ALL = ROW + COL


def matmul(a, b, dims=((1,), (0,)), precision=lax.Precision.HIGHEST):
    return lax.dot_general(a, b, (dims, ((), ())), precision=precision, preferred_element_type=jnp.float32)


def row_depth(block_depth, first_row, row_total):
    blocks = (first_row + jnp.arange(row_total, dtype=jnp.int32)) // BLOCK
    block_ids = jnp.arange(block_depth.shape[0], dtype=jnp.int32)
    matched = (blocks[:, None] == block_ids[None, :]).astype(jnp.int32)
    return jnp.sum(matched * block_depth[None, :], axis=1)


def shards(sigma_top, panel, parent_panel, diag_inverse, block_depth):
    rows_n, cols_n = lax.axis_size(ROW), lax.axis_size(COL)
    r, c = lax.axis_index(ROW), lax.axis_index(COL)
    steps, share, width = panel.shape
    group = sigma_top.shape[1]
    part = width // rows_n
    depth = row_depth(block_depth, (r * cols_n + c) * share, share)
    masks = [jnp.where(depth > k, 1.0, 0.0).astype(jnp.float32)[:, None] for k in range(steps)]

    n = []
    for k in range(steps):
        value = masks[k] * panel[k]
        if k:
            value = value - matmul(n[-1], parent_panel[k - 1])
        n.append(value)
    natural = jnp.concatenate(n, axis=1)
    sliced = jnp.stack(n, 1).reshape(share, steps, rows_n, part).transpose(0, 2, 1, 3).reshape(share, steps * width)

    to_group = [(i * cols_n + j, (j % rows_n) * cols_n + i * (cols_n // rows_n) + j // rows_n)
                for i in range(rows_n) for j in range(cols_n)]
    moved = lax.ppermute(natural, ALL, to_group)
    group_n = lax.all_gather(moved, ROW, axis=0, tiled=True)

    gathered = lax.all_gather(sliced, COL, axis=0, tiled=True)
    partial = matmul(gathered, sigma_top, ((0,), (0,)))
    y = lax.psum_scatter(partial, ROW, scatter_dimension=0, tiled=True).reshape(steps, part, group)

    grams = []
    for k in range(steps):
        grams.append(matmul(y[k], group_n[:, k * width:(k + 1) * width]))
    for k in range(1, steps):
        grams.append(matmul(y[k - 1], group_n[:, k * width:(k + 1) * width]))
    count = len(grams)
    z_n, x_n = lax.axis_size("z"), lax.axis_size("x")
    tiles = jnp.stack(grams).reshape(count, z_n, part // z_n, x_n, width // x_n).transpose(1, 3, 0, 2, 4)
    tiles = tiles.reshape((cols_n,) + tiles.shape[2:])
    mine = jnp.sum(lax.all_to_all(tiles, COL, 0, 0, tiled=True), axis=0)
    every = lax.all_to_all(jnp.broadcast_to(mine[None], (cols_n,) + mine.shape), COL, 0, 0, tiled=True)
    every = every.reshape((z_n, x_n) + mine.shape).transpose(2, 0, 3, 1, 4).reshape(count, part, width)

    start = r * part
    diags, links = [], []
    inner = None
    for k in range(steps):
        inverse = diag_inverse[k]
        if k < steps - 1:
            full = matmul(inverse, inverse, ((0,), (0,)))
            if k:
                full = full + matmul(parent_panel[k - 1], inner, ((0,), (0,)))
            own = lax.dynamic_slice_in_dim(full, start, part, 0)
            inner = matmul(full, parent_panel[k])
            links.append(every[steps + k] - lax.dynamic_slice_in_dim(inner, start, part, 0))
        else:
            own = matmul(lax.dynamic_slice_in_dim(inverse, start, part, 1), inverse, ((0,), (0,)))
            if k:
                own = own + matmul(lax.dynamic_slice_in_dim(parent_panel[k - 1], start, part, 1), inner, ((0,), (0,)))
        diags.append(own + every[k])

    blocks = y.reshape(steps, part, rows_n, share).transpose(2, 0, 3, 1)
    blocks = blocks.reshape(rows_n, steps * share * part // width, width)
    blocks = lax.all_to_all(blocks, ROW, 0, 0, tiled=True)
    mine_y = blocks.reshape(rows_n, steps, share, part).transpose(1, 2, 0, 3).reshape(steps, share, width)
    own_y = lax.ppermute(mine_y, ALL, [(b, a) for a, b in to_group])
    cols = jnp.stack([-masks[k] * own_y[k] for k in range(steps)])
    return cols, jnp.stack(links), jnp.stack(diags)


def solution(mesh):
    axes = Mesh(mesh.devices.reshape(4, 2, 8, 4), ("y", "core", "z", "x"))
    return jax.shard_map(
        shards,
        mesh=axes,
        in_specs=(P(ROW, COL), P(None, ALL, None), P(), P(), P()),
        out_specs=(P(None, ALL, None), P(None, ROW, None), P(None, ROW, None)),
        check_vma=False,
    )
```

time: 1590 us -> 312 us (0.20)
  waiting for transfers between devices: 1480 us -> 181 us
  starting transfers between devices: 0.79 us -> 33.8 us
    reduce_scatter x3 -> x1, waiting for transfers between devices: 639 us -> 36.7 us  [shards(): lax.psum_scatter(partial, ROW, scatter_dimension=0, tiled=True)]
    psum x2 -> x0, waiting for transfers between devices: 334 us -> none  [the longest x1 265 us: shards(): crossed = lax.psum(cross_parts[section - 1], ('row', 'col'))]
    all_gather x4 -> x2, waiting for transfers between devices: 307 us -> 84.1 us  [the longest x1 71.1 us: shards(): gathered = lax.all_gather(sliced, COL, axis=0, tiled=True)]
    unnamed x11 -> x3, waiting for transfers between devices: 199 us -> 0.05 us
    ppermute x0 -> x2, waiting for transfers between devices: none -> 50.1 us  [the longest x1 27.2 us: shards(): moved = lax.ppermute(natural, ALL, to_group)]
    all_to_all x0 -> x3, starting transfers between devices: none -> 22.4 us  [the longest x1 10.2 us: shards(): mine = jnp.sum(lax.all_to_all(tiles, COL, 0, 0, tiled=True), axis=0)]
    dot_general x24 -> x21, matrix products: 67.2 us -> 58.7 us  [matmul(): lax.dot_general(a, b, (dims, ((), ())), precision=precision, preferred_el...]
  transfers between devices with their start and end apart: 10 -> 8, of which waited for: 10 -> 7; matrix products, arithmetic and copies ran while one was open for 4% -> 18% of each run, Pallas kernels for 0% -> 0%
where the time goes in v1:
time: 312 us; the launch traced here: 310 us
  waiting for transfers between devices  181 us (58%)
  matrix products  58.7 us (19%)
  starting transfers between devices  33.8 us (11%)
  local copies, waits for them, and re-layouts  15.4 us (5%)
  between operations  14.1 us (5%)
  other arithmetic  7.44 us (2%)
    all_gather x1, waiting for transfers between devices, shards(): gathered = lax.all_gather(sliced, COL, axis=0, tiled=True)  71.1 us
    dot_general x21, matrix products, matmul(): lax.dot_general(a, b, (dims, ((), ())), precision=precision, preferred_el...  58.7 us
    reduce_scatter x1, waiting for transfers between devices, shards(): lax.psum_scatter(partial, ROW, scatter_dimension=0, tiled=True)  36.7 us
    ppermute x1, waiting for transfers between devices, shards(): moved = lax.ppermute(natural, ALL, to_group)  27.2 us
    ppermute x1, waiting for transfers between devices, shards(): own_y = lax.ppermute(mine_y, ALL, [(b, a) for a, b in to_group])  22.9 us
    all_gather x1, waiting for transfers between devices, shards(): group_n = lax.all_gather(moved, ROW, axis=0, tiled=True)  13.1 us
    all_to_all x1, starting transfers between devices, shards(): mine = jnp.sum(lax.all_to_all(tiles, COL, 0, 0, tiled=True), axis=0)  10.2 us
    all_to_all x1, waiting for transfers between devices, shards(): mine = jnp.sum(lax.all_to_all(tiles, COL, 0, 0, tiled=True), axis=0)  8.92 us
  transfers between devices with their start and end apart: 8, of which 7 were waited for; matrix products, arithmetic and copies ran while one was open for 18% of the time, Pallas kernels for 0%

profile of v1, /device:TPU:44, one launch (start us, length us, event | category | flops | bytes accessed | tf_op | source)
XLA Modules:
  0.0 310.4 jit_solution(6500098132460355138)
XLA Ops:
  7.3 0.9 select_reduce_fusion
  8.2 2.0 convolution_subtract_fusion.2
  10.2 0.1 stack.71
  10.3 2.0 convolution_subtract_fusion.1
  12.2 0.1 stack.72
  12.3 1.9 convolution_subtract_fusion
  14.3 0.1 stack.73
  14.4 0.1 squeeze.73
  14.4 0.1 broadcast_multiply_fusion
  14.6 0.1 copy.39
  14.7 1.1 reshape.180
  15.9 0.0 all-gather.5.cloned.1.call-start
  16.0 0.1 bitcast_multiply_fusion
  16.1 5.5 %collective-permute-start.1 = (f32[32,2048]{1,0:T(8,128)S(1)}, f32[32,2048]{1,0:T(8,128)S(1)}, u32[]{:S(2)}, u32[]{:S(2)}) collective-permute-start(f32[32,2048]{1,0:T(8,128)S(1)} %pad_maximum_fusion.3), channel_id=1, source_target_pairs={{0,0},{1,32},{2,64},{3,96},{4,128},{5,160},{6,192},{7,224},{8,1},{... | collective-permute-start | bytes 786440 | tf_op jit(solution)/shard_map/ppermute | solution.py:43
  21.6 27.2 %collective-permute-done.1 = f32[32,2048]{1,0:T(8,128)S(1)} collective-permute-done((f32[32,2048]{1,0:T(8,128)S(1)}, f32[32,2048]{1,0:T(8,128)S(1)}, u32[]{:S(2)}, u32[]{:S(2)}) %collective-permute-start.1) | collective-permute-done | bytes 262176 | tf_op jit(solution)/shard_map/ppermute | solution.py:43
  48.7 0.7 copy-done.12
  49.5 0.0 reduce-scatter.2.cloned.1.call-start
  49.5 71.1 %all-gather.3.cloned.1.call-done = f32[1024,2048]{1,0:T(8,128)} async-done(((f32[32,2048]{1,0:T(8,128)}), f32[1024,2048]{1,0:T(8,128)}) %all-gather.3.cloned.1.call-update) | async-done | bytes 8388624 | tf_op jit(solution)/shard_map/all_gather | solution.py:46
  120.6 16.6 %fusion.81 = f32[2048,256]{1,0:T(8,128)} fusion(f32[1024,2048]{1,0:T(8,128)} %all-gather.3.cloned.1.call-done, f32[1024,256]{1,0:T(8,128)S(1)} %copy-done), kind=kOutput, calls=%fused_computation.126 | convolution fusion | flops 6442450944 | bytes 11534336 | tf_op jit(solution)/shard_map/dot_general | solution.py:13
  137.2 13.1 %all-gather.5.cloned.1.call-done = f32[256,2048]{1,0:T(8,128)} async-done(((f32[32,2048]{1,0:T(8,128)}), f32[256,2048]{1,0:T(8,128)}) %all-gather.5.cloned.1.call-update) | async-done | bytes 2097168 | tf_op jit(solution)/shard_map/all_gather | solution.py:44
  150.2 36.7 %reduce-scatter.2.cloned.1.call-done = f32[256,256]{1,0:T(8,128)} async-done(((f32[2048,256]{1,0:T(8,128)}), f32[256,256]{1,0:T(8,128)}) %reduce-scatter.2.cloned.1.call-update) | async-done | bytes 262160 | tf_op jit(solution)/shard_map/reduce_scatter | solution.py:48
  187.0 1.5 fusion.8
  188.5 1.5 fusion.7
  190.0 1.5 fusion.6
  191.6 1.5 fusion.5
  193.1 1.3 fusion.4
  194.4 0.4 fusion.3
  194.8 0.4 fusion.2
  195.2 1.0 copy.43
  196.2 10.2 %all-to-all-start.1 = ((f32[32,7,8,128]{3,2,1,0:T(8,128)}), f32[32,7,8,128]{3,2,1,0:T(8,128)S(1)}, u32[]{:S(2)}, u32[]{:S(2)}) async-start(f32[32,7,8,128]{3,2,1,0:T(8,128)} %bitcast.19), calls=%async_computation.2 | async-start | bytes 1835008 | tf_op jit(solution)/shard_map/all_to_all | solution.py:59
  206.5 3.5 %fusion.17 = f32[512,512]{1,0:T(8,128)S(1)} fusion(f32[4,512,512]{2,1,0:T(8,128)} %param.8), kind=kOutput, calls=%fused_computation.30 | convolution fusion | flops 1610612736 | bytes 2097152 | tf_op jit(solution)/shard_map/dot_general | solution.py:13
  210.0 4.8 %fusion.15 = f32[512,512]{1,0:T(8,128)} fusion(f32[4,512,512]{2,1,0:T(8,128)} %param.8), kind=kOutput, calls=%fused_computation.28 | convolution fusion | flops 1610612736 | bytes 2097152 | tf_op jit(solution)/shard_map/dot_general | solution.py:13
  214.8 1.8 fusion.27
  216.7 1.0 copy.40
  217.7 1.2 reshape_reshape.3
  218.8 0.9 copy.41
  219.7 1.9 reshape.181
  221.6 8.9 %all-to-all-done.1 = f32[32,7,8,128]{3,2,1,0:T(8,128)S(1)} async-done(((f32[32,7,8,128]{3,2,1,0:T(8,128)}), f32[32,7,8,128]{3,2,1,0:T(8,128)S(1)}, u32[]{:S(2)}, u32[]{:S(2)}) %all-to-all-start.1) | async-done | bytes 917536 | tf_op jit(solution)/shard_map/all_to_all | solution.py:59
  230.5 0.9 copy-done.9
  231.4 6.1 %all-to-all-start = ((f32[8,16,512]{2,1,0:T(8,128)}), f32[8,16,512]{2,1,0:T(8,128)S(1)}, u32[]{:S(2)}, u32[]{:S(2)}) async-start(f32[8,16,512]{2,1,0:T(8,128)} %reshape.181), calls=%async_computation.1 | async-start | bytes 524288 | tf_op jit(solution)/shard_map/all_to_all | solution.py:83
  237.6 3.4 %fusion.1 = f32[512,512]{1,0:T(8,128)S(1)} fusion(f32[512,512]{1,0:T(8,128)} %fusion.15, f32[512,512]{1,0:T(8,128)S(1)} %fusion.27, f32[3,512,512]{2,1,0:T(8,128)} %param.7), kind=kOutput, calls=%fused_computation.3 | convolution fusion | flops 1610874880 | bytes 4194304 | tf_op jit(solution)/shard_map/dot_general | solution.py:13
  241.0 1.6 reduce_sum.19
  242.6 1.0 all-to-all-done
  243.6 1.0 broadcast_in_dim.29
  244.7 6.1 %all-to-all-start.2 = ((f32[32,7,8,128]{3,2,1,0:T(8,128)}), f32[32,7,8,128]{3,2,1,0:T(8,128)}, u32[]{:S(2)}, u32[]{:S(2)}) async-start(f32[32,7,8,128]{3,2,1,0:T(8,128)} %broadcast_in_dim.29), calls=%async_computation.3 | async-start | bytes 1835008 | tf_op jit(solution)/shard_map/all_to_all | solution.py:60
  250.8 3.5 %fusion.13 = f32[512,512]{1,0:T(8,128)S(1)} fusion(f32[4,512,512]{2,1,0:T(8,128)} %param.8), kind=kOutput, calls=%fused_computation.26 | convolution fusion | flops 1610612736 | bytes 2097152 | tf_op jit(solution)/shard_map/dot_general | solution.py:13
  254.3 3.1 fusion.23
  257.4 1.0 copy-done.7
  258.4 1.9 fusion
  260.3 0.1 reshape.182
  260.5 0.3 copy.42
  260.8 0.1 reshape.183
  260.9 5.8 %collective-permute-start = (f32[4,32,512]{2,1,0:T(8,128)S(1)}, f32[4,32,512]{2,1,0:T(8,128)}, u32[]{:S(2)}, u32[]{:S(2)}) collective-permute-start(f32[4,32,512]{2,1,0:T(8,128)S(1)} %reshape.183), channel_id=1, source_target_pairs={{0,0},{32,1},{64,2},{96,3},{128,4},{160,5},{192,6},{224,7},{1,8},{... | collective-permute-start | bytes 786440 | tf_op jit(solution)/shard_map/ppermute | solution.py:85
  266.7 3.1 fusion.19
  269.8 2.3 slice.141
  272.1 2.1 fusion.11
  274.2 22.9 %collective-permute-done = f32[4,32,512]{2,1,0:T(8,128)} collective-permute-done((f32[4,32,512]{2,1,0:T(8,128)S(1)}, f32[4,32,512]{2,1,0:T(8,128)}, u32[]{:S(2)}, u32[]{:S(2)}) %collective-permute-start) | collective-permute-done | bytes 262176 | tf_op jit(solution)/shard_map/ppermute | solution.py:85
  297.2 1.0 slice_multiply_fusion.3
  298.2 0.7 pad_maximum_fusion.2
  298.9 1.3 copy.46
  300.2 1.3 fusion.55
  301.5 0.8 fusion.10
  302.3 0.8 pad_maximum_fusion.1
  303.1 0.8 pad_maximum_fusion
  (36 shorter events, 0.2 us)
Async XLA Ops:
  7.2 113.4 %copy-start = (f32[1024,256]{1,0:T(8,128)S(1)}, f32[1024,256]{1,0:T(8,128)}, u32[]{:S(2)}) copy-start(f32[1024,256]{1,0:T(8,128)} %param.5) | copy-start | bytes 3145732
  7.2 7.2 %slice-start.1 = ((f32[4,32,512]{2,1,0:T(8,128)}), f32[1,32,512]{2,1,0:T(8,128)S(1)}, s32[]{:S(2)}) async-start(f32[4,32,512]{2,1,0:T(8,128)} %param.6), calls=%async_computation.8 | async-start | bytes 131072 | tf_op jit(solution)/shard_map/slice | solution.py:34
  7.2 113.4 %all-gather.3.cloned.1.call-start = ((), (), s32[]{:S(2)}) async-start(), calls=%async_computation.4 | async-start | bytes 8650752 | tf_op jit(solution)/shard_map/all_gather | solution.py:46
  10.2 5.7 %copy-start.11 = (f32[4,32,512]{2,1,0:T(8,128)S(1)}, f32[4,32,512]{2,1,0:T(8,128)}, u32[]{:S(2)}) copy-start(f32[4,32,512]{2,1,0:T(8,128)} %param.6) | copy-start | bytes 786436
  15.9 134.3 %all-gather.5.cloned.1.call-start = ((), (), s32[]{:S(2)}) async-start(), calls=%async_computation.6 | async-start | bytes 2359296 | tf_op jit(solution)/shard_map/all_gather | solution.py:44
  16.1 32.7 %collective-permute-start.1 = (f32[32,2048]{1,0:T(8,128)S(1)}, f32[32,2048]{1,0:T(8,128)S(1)}, u32[]{:S(2)}, u32[]{:S(2)}) collective-permute-start(f32[32,2048]{1,0:T(8,128)S(1)} %pad_maximum_fusion.3), channel_id=1, source_target_pairs={{0,0},{1,32},{2,64},{3,96},{4,128},{5,160},{6,192},{7,224},{8,1},{... | collective-permute-start | bytes 786440 | tf_op jit(solution)/shard_map/ppermute | solution.py:43
  48.7 0.7 copy-start.12
  49.5 137.5 %reduce-scatter.2.cloned.1.call-start = ((), (), s32[]{:S(2)}) async-start(), calls=%async_computation.5 | async-start | bytes 2359296 | tf_op jit(solution)/shard_map/reduce_scatter | solution.py:48
  150.2 42.9 %copy-start.3 = (f32[256,2048]{1,0:T(8,128)S(1)}, f32[256,2048]{1,0:T(8,128)}, u32[]{:S(2)}) copy-start(f32[256,2048]{1,0:T(8,128)} %all-gather.5.cloned.1.call-done) | copy-start | bytes 6291460
  187.0 7.4 %copy-start.10 = (f32[256,256]{1,0:T(8,128)S(1)}, f32[256,256]{1,0:T(8,128)}, u32[]{:S(2)}) copy-start(f32[256,256]{1,0:T(8,128)} %reduce-scatter.2.cloned.1.call-done) | copy-start | bytes 786436
  196.2 34.3 %all-to-all-start.1 = ((f32[32,7,8,128]{3,2,1,0:T(8,128)}), f32[32,7,8,128]{3,2,1,0:T(8,128)S(1)}, u32[]{:S(2)}, u32[]{:S(2)}) async-start(f32[32,7,8,128]{3,2,1,0:T(8,128)} %bitcast.19), calls=%async_computation.2 | async-start | bytes 1835008 | tf_op jit(solution)/shard_map/all_to_all | solution.py:59
  206.5 8.3 %copy-start.1 = (f32[3,512,512]{2,1,0:T(8,128)S(1)}, f32[3,512,512]{2,1,0:T(8,128)}, u32[]{:S(2)}) copy-start(f32[3,512,512]{2,1,0:T(8,128)} %param.7) | copy-start | bytes 9437188
  210.0 4.8 %copy-start.4 = (f32[512,512]{1,0:T(8,128)}, f32[512,512]{1,0:T(8,128)S(1)}, u32[]{:S(2)}) copy-start(f32[512,512]{1,0:T(8,128)S(1)} %fusion.17) | copy-start | bytes 3145732
  216.7 24.3 %copy-start.5 = (f32[512,512]{1,0:T(8,128)}, f32[512,512]{1,0:T(8,128)S(1)}, u32[]{:S(2)}) copy-start(f32[512,512]{1,0:T(8,128)S(1)} %fusion.27) | copy-start | bytes 3145732
  230.5 0.9 copy-start.9
  231.4 12.2 %all-to-all-start = ((f32[8,16,512]{2,1,0:T(8,128)}), f32[8,16,512]{2,1,0:T(8,128)S(1)}, u32[]{:S(2)}, u32[]{:S(2)}) async-start(f32[8,16,512]{2,1,0:T(8,128)} %reshape.181), calls=%async_computation.1 | async-start | bytes 524288 | tf_op jit(solution)/shard_map/all_to_all | solution.py:83
  241.0 16.4 %copy-start.6 = (f32[512,512]{1,0:T(8,128)}, f32[512,512]{1,0:T(8,128)S(1)}, u32[]{:S(2)}) copy-start(f32[512,512]{1,0:T(8,128)S(1)} %fusion.1) | copy-start | bytes 3145732
  244.7 54.2 %all-to-all-start.2 = ((f32[32,7,8,128]{3,2,1,0:T(8,128)}), f32[32,7,8,128]{3,2,1,0:T(8,128)}, u32[]{:S(2)}, u32[]{:S(2)}) async-start(f32[32,7,8,128]{3,2,1,0:T(8,128)} %broadcast_in_dim.29), calls=%async_computation.3 | async-start | bytes 1835008 | tf_op jit(solution)/shard_map/all_to_all | solution.py:60
  250.8 7.7 %copy-start.2 = (f32[3,512,512]{2,1,0:T(8,128)S(1)}, f32[3,512,512]{2,1,0:T(8,128)}, u32[]{:S(2)}) copy-start(f32[3,512,512]{2,1,0:T(8,128)} %param.7) | copy-start | bytes 9437188
  257.4 1.0 copy-start.7
  260.3 11.8 %copy-start.8 = (f32[512,512]{1,0:T(8,128)}, f32[512,512]{1,0:T(8,128)S(1)}, u32[]{:S(2)}) copy-start(f32[512,512]{1,0:T(8,128)S(1)} %fusion) | copy-start | bytes 3145732
  260.9 36.2 %collective-permute-start = (f32[4,32,512]{2,1,0:T(8,128)S(1)}, f32[4,32,512]{2,1,0:T(8,128)}, u32[]{:S(2)}, u32[]{:S(2)}) collective-permute-start(f32[4,32,512]{2,1,0:T(8,128)S(1)} %reshape.183), channel_id=1, source_target_pairs={{0,0},{32,1},{64,2},{96,3},{128,4},{160,5},{192,6},{224,7},{1,8},{... | collective-permute-start | bytes 786440 | tf_op jit(solution)/shard_map/ppermute | solution.py:85
  272.1 29.4 %slice-start = ((f32[3,512,512]{2,1,0:T(8,128)}), f32[1,512,512]{2,1,0:T(8,128)S(1)}, s32[]{:S(2)}) async-start(f32[3,512,512]{2,1,0:T(8,128)} %param.7), calls=%async_computation.7 | async-start | bytes 2097152 | tf_op jit(solution)/shard_map/slice | solution.py:36
Sparse Core Ops, SparseCore 0:
  16.0 104.5 all-gather.2
  123.0 27.1 all-gather.4
  152.8 34.1 reduce-scatter.1
